TPU v7x, 512 devices: a whole 4x8x8 slice. The times are simulated.
512 devices in a mesh: tile: 128 (over z, y, core), grp: 4 (over x).
Axes of the slice: x: 4, y: 8, z: 8, core: 2. Of those that a mesh axis runs over, the one named last changes fastest.
Arguments:
- kelvin_profile: float32 [90, 128, 256], P(None, 'tile'), may hold values from 0.5 to 1.5
- moisture_profile: float32 [90, 128, 256], P(None, 'tile'), may hold values from 0.1 to 3
- spreading_number: float32 [128, 256], P('tile'), may hold values from 0.05 to 0.24
- overhead_angle_measure: float32 [128, 256], P('tile'), may hold values from 0.2 to 1
- illuminated_mask: int32 [128, 256], P('tile'), may hold values 0 or 1
- radiating_tiles: int32 [32768, 1], P('tile'), may hold values from 0 to 127; in each aligned block of 256 rows (0 to 255, 256 to 511, ...) at most 4 rows name the same one
- cloudy_member_factors: float32 [224, 65536], P('grp', 'tile'), may hold values from 0.25 to 2
- arid_opacity_table: float32 [224, 90], P('grp'), may hold values from 0.003 to 0.2
- moisture_attenuation: float32 [224], P('grp'), may hold values from 0.003 to 0.05
- blackbody_share: float32 [224], P('grp'), may hold values from 0.3 to 3
- insolation_per_quadrature: float32 [224], P('grp'), may hold values from 0.3 to 3
Outputs:
- heating: float32 [90, 128, 256], P(None, 'tile')
- temp_next: float32 [90, 128, 256], P(None, 'tile')
- vapour_next: float32 [90, 128, 256], P(None, 'tile')
Inputs may be any that keep to these rules, and one draw needn't show every extreme that they name: `radiating_tiles`: among the columns of one tile no owner is named more than 4 times, a bound that some block reaches.
All inputs are finite; a program needn't handle non-finite values. No bound on the sum of `illuminated_mask` on one device may be relied on, other than what follows from the above.
Results may differ from a plain program's by a relative error of at most 0.00025.
Values sent between devices are 32-bit elements; how exact they have to be, the bound alone decides.
A program may use at most 64 MiB of HBM per device.

v0:
```python
import math
import jax
import jax.numpy as jnp
from jax import lax
from jax.sharding import PartitionSpec as P

NG = 224


def with_halo(block, sides, width):
    for axis, dim in sides:
        count = lax.axis_size(axis)
        forward = [(i, i + 1) for i in range(count - 1)]
        backward = [(target, source) for source, target in forward]
        low = lax.ppermute(
            lax.slice_in_dim(block, block.shape[dim] - width, None, axis=dim), axis, forward
        )
        high = lax.ppermute(lax.slice_in_dim(block, 0, width, axis=dim), axis, backward)
        block = jnp.concatenate([low, block, high], axis=dim)
    return block


def evaluate_warming(
    kelvin_profile,
    moisture_profile,
    overhead_angle_value,
    illuminated_marker,
    profile_window,
    arid_multiplier,
    moisture_multiplier,
    radiance_share_table,
    sunshine_multiplier,
):
    gpoints, strata_mesh = arid_multiplier.shape
    bundle = math.gcd(gpoints, 4)
    bundles = gpoints // bundle
    lower_mask = (jnp.arange(strata_mesh)[None, :] < jnp.arange(strata_mesh + 1)[:, None]).astype(
        jnp.float32
    )
    upper_mask = 1.0 - lower_mask

    def layer_pass(pieces):
        dry_part, vapour_part, radiance_share_piece, solar_part, sub_part = pieces
        thickness = (
            dry_part[:, :, None]
            + (vapour_part[:, None] * sub_part)[:, None, :] * moisture_profile[None]
        )
        column_depth = jnp.einsum(
            "lk,gkm->glm", lower_mask, thickness, precision=lax.Precision.HIGHEST
        )
        growth = jnp.exp(column_depth)
        damped = jnp.exp(-column_depth)
        infrared_radiance = radiance_share_piece[:, None, None] * kelvin_profile[None]
        downward = damped * jnp.einsum(
            "lk,gkm->glm",
            lower_mask,
            infrared_radiance * growth[:, :strata_mesh] * jnp.expm1(thickness),
            precision=lax.Precision.HIGHEST,
        )
        floor_term = infrared_radiance[:, strata_mesh - 1] * damped[:, strata_mesh]
        upward = growth * (
            floor_term[:, None, :]
            - jnp.einsum(
                "lk,gkm->glm",
                upper_mask,
                infrared_radiance * damped[:, :strata_mesh] * jnp.expm1(-thickness),
                precision=lax.Precision.HIGHEST,
            )
        )
        sunbeam = (
            solar_part[:, None, None]
            * illuminated_marker[None, None, :]
            * jnp.exp(-column_depth / overhead_angle_value[None, None, :])
        )
        fluxes = downward - upward + sunbeam
        return jnp.sum(fluxes[:, :strata_mesh] - fluxes[:, 1:], axis=0)

    spectral = lax.map(
        layer_pass,
        (
            arid_multiplier.reshape(bundles, bundle, strata_mesh),
            moisture_multiplier.reshape(bundles, bundle),
            radiance_share_table.reshape(bundles, bundle),
            sunshine_multiplier.reshape(bundles, bundle),
            profile_window.reshape(bundles, bundle, profile_window.shape[1]),
        ),
    )
    return jnp.sum(spectral, axis=0)


def advance(atmosphere_variables, spreading_number):
    padded = with_halo(atmosphere_variables, (("tile", 2),), 1)
    eastern = jnp.roll(atmosphere_variables, -1, axis=3)
    western = jnp.roll(atmosphere_variables, 1, axis=3)
    return atmosphere_variables + spreading_number * (
        padded[:, :, :-2] + padded[:, :, 2:] + eastern + western - 4.0 * atmosphere_variables
    )


def on_device(
    kelvin_profile,
    moisture_profile,
    spreading_number,
    overhead_angle_measure,
    illuminated_mask,
    radiating_tiles,
    cloudy_member_factors,
    arid_opacity_table,
    moisture_attenuation,
    blackbody_share,
    insolation_per_quadrature,
):
    strata_mesh, parallel_band_sequence, meridian_boxes = kelvin_profile.shape
    atmosphere_variables = jnp.stack([kelvin_profile, moisture_profile])
    for repeat in range(2):
        atmosphere_variables = advance(atmosphere_variables, spreading_number)
    temp_dyn = atmosphere_variables[0]
    vapour_next = atmosphere_variables[1]
    columns = parallel_band_sequence * meridian_boxes
    tile_count = lax.axis_size("tile")
    capacity = cloudy_member_factors.shape[1] // tile_count
    slots = tile_count * capacity
    owner_ids = radiating_tiles[:, 0]
    matches = (owner_ids[:, None] == jnp.arange(tile_count, dtype=jnp.int32)[None, :]).astype(
        jnp.int32
    )
    position = jnp.sum((jnp.cumsum(matches, axis=0) - 1) * matches, axis=1)
    slot_index = owner_ids * capacity + position
    overhead_angle_value = overhead_angle_measure.reshape(columns)
    sunlit_local = overhead_angle_value * illuminated_mask.reshape(columns).astype(jnp.float32)
    column_rows = jnp.concatenate(
        [temp_dyn.reshape(strata_mesh, columns).T, vapour_next.reshape(strata_mesh, columns).T],
        axis=1,
    )
    outgoing = (
        jnp.zeros((slots, 2 * strata_mesh), jnp.float32)
        .at[slot_index]
        .set(column_rows)
        .reshape(tile_count, capacity, 2 * strata_mesh)
    )
    sun_rows = jnp.stack([overhead_angle_value, sunlit_local], axis=1)
    blank = jnp.stack([jnp.ones((slots,), jnp.float32), jnp.zeros((slots,), jnp.float32)], axis=1)
    sun_out = blank.at[slot_index].set(sun_rows).reshape(tile_count, capacity, 2)
    incoming, sun_in = (
        lax.all_to_all(outgoing, "tile", split_axis=0, concat_axis=0, tiled=True),
        lax.all_to_all(sun_out, "tile", split_axis=0, concat_axis=0, tiled=True),
    )
    incoming = incoming.reshape(slots, 2 * strata_mesh)
    sun_in = sun_in.reshape(slots, 2)
    partial_value = evaluate_warming(
        incoming[:, :strata_mesh].T,
        incoming[:, strata_mesh:].T,
        sun_in[:, 0],
        sun_in[:, 1],
        cloudy_member_factors,
        arid_opacity_table,
        moisture_attenuation,
        blackbody_share,
        insolation_per_quadrature,
    )
    summed = lax.psum(partial_value, "grp")
    returning = lax.all_to_all(
        summed.T.reshape(tile_count, capacity, strata_mesh),
        "tile",
        split_axis=0,
        concat_axis=0,
        tiled=True,
    )
    total_heat = returning.reshape(slots, strata_mesh)[slot_index].T
    heating = (total_heat / NG).reshape(strata_mesh, parallel_band_sequence, meridian_boxes)
    return (heating, temp_dyn + heating, vapour_next)


def solution(mesh):
    in_specs = (
        P(None, "tile", None),
        P(None, "tile", None),
        P("tile", None),
        P("tile", None),
        P("tile", None),
        P("tile", None),
        P("grp", "tile"),
        P("grp", None),
        P("grp"),
        P("grp"),
        P("grp"),
    )
    out_specs = (P(None, "tile", None), P(None, "tile", None), P(None, "tile", None))
    return jax.shard_map(
        on_device, mesh=mesh, in_specs=in_specs, out_specs=out_specs, check_vma=False
    )
```

profile of v0, /device:TPU:1, one launch (start us, length us, event | category | flops | bytes accessed | tf_op | source)
XLA Modules:
  0.0 282.9 jit_solution(3957127956137913107)
XLA Ops:
  9.2 8.8 %collective-permute-start.1 = (f32[2,90,1,256]{1,3,2,0:T(8,128)S(1)}, f32[2,90,1,256]{1,3,2,0:T(8,128)S(1)}, u32[]{:S(2)}, u32[]{:S(2)}) collective-permute-start(f32[2,90,1,256]{1,3,2,0:T(8,128)S(1)} %pad_maximum_fusion), channel_id=1, source_target_pairs={{4,0},{8,4},{12,8},{16,12},{20,16},{24,20},{28,24},{32,28},{36,32}... | collective-permute-start | bytes 552968 | tf_op jit(solution)/shard_map/ppermute | solution.py:18
  18.0 1.9 collective-permute-start
  25.5 1.5 copy.61
  27.0 12.7 %all-to-all-start.1 = ((f32[128,4,2]{1,2,0:T(2,128)}), f32[128,4,2]{1,2,0:T(2,128)S(1)}, u32[]{:S(2)}, u32[]{:S(2)}) async-start(f32[128,4,2]{1,2,0:T(2,128)} %copy.61), calls=%async_computation.1 | async-start | bytes 262144 | tf_op jit(solution)/shard_map/all_to_all | solution.py:146
  39.9 2.8 collective-permute-start.3
  42.7 2.8 collective-permute-start.2
  45.5 2.3 collective-permute-done.3
  48.9 1.7 scatter_custom_fusion
  52.4 15.6 %all-to-all-start = ((f32[128,4,180]{2,1,0:T(4,128)}), f32[128,4,180]{2,1,0:T(4,128)}, u32[]{:S(2)}, u32[]{:S(2)}) async-start(f32[128,4,180]{2,1,0:T(4,128)} %reshape.191), calls=%async_computation | async-start | bytes 1048576 | tf_op jit(solution)/shard_map/all_to_all | solution.py:145
  71.0 1.6 reshape.189
  74.2 14.0 %all-to-all-done = f32[128,4,180]{2,1,0:T(4,128)} async-done(((f32[128,4,180]{2,1,0:T(4,128)}), f32[128,4,180]{2,1,0:T(4,128)}, u32[]{:S(2)}, u32[]{:S(2)}) %all-to-all-start) | async-done | bytes 368672 | tf_op jit(solution)/shard_map/all_to_all | solution.py:145
  88.2 2.0 reshape.192
  90.2 2.0 slice_bitcast_fusion
  94.4 103.7 %while.12 = (s32[]{:T(128)}, f32[14,90,512]{2,1,0:T(8,128)S(1)}, f32[14,4,90]{2,1,0:T(4,128)}, f32[14,4]{1,0:T(8,128)S(1)}, f32[14,4,512]{2,1,0:T(4,128)}, /*ind...) while((s32[]{:T(128)}, f32[14,90,512]{2,1,0:T(8,128)S(1)}, ...), condition=%wide.region_7.8_spmd.clone.clone, body=%wide.region_5.7_spmd.clone.clone.sunk | while | flops 608476160 | bytes 12221821 | solution.py:78
  100.2 1.5 fusion.81
  107.6 1.5 fusion.81
  115.0 1.5 fusion.81
  122.4 1.5 fusion.81
  129.8 1.5 fusion.81
  137.2 1.5 fusion.81
  144.6 1.5 fusion.81
  152.0 1.5 fusion.81
  159.4 1.5 fusion.81
  166.8 1.5 fusion.81
  172.8 1.4 fusion.79
  174.2 1.5 fusion.81
  181.6 1.5 fusion.81
  189.0 1.5 fusion.81
  196.4 1.5 fusion.81
  199.2 42.9 %all-reduce.2.cloned.1.call-done = f32[128,4,90]{2,1,0:T(4,128)} async-done(((f32[128,4,90]{2,1,0:T(4,128)}), f32[128,4,90]{2,1,0:T(4,128)}) %all-reduce.2.cloned.1.call-update) | async-done | bytes 184336 | tf_op jit(solution)/shard_map/psum | solution.py:161
  242.1 16.4 %all-to-all-start.2 = ((f32[128,4,90]{2,1,0:T(4,128)}), f32[128,4,90]{2,1,0:T(4,128)S(1)}, u32[]{:S(2)}, u32[]{:S(2)}) async-start(f32[128,4,90]{2,1,0:T(4,128)} %all-reduce.2.cloned.1.call-done), calls=%async_computation.2 | async-start | bytes 524288 | tf_op jit(solution)/shard_map/all_to_all | solution.py:162
  259.3 14.5 %all-to-all-done.2 = f32[128,4,90]{2,1,0:T(4,128)S(1)} async-done(((f32[128,4,90]{2,1,0:T(4,128)}), f32[128,4,90]{2,1,0:T(4,128)S(1)}, u32[]{:S(2)}, u32[]{:S(2)}) %all-to-all-start.2) | async-done | bytes 184352 | tf_op jit(solution)/shard_map/all_to_all | solution.py:162
  (265 shorter events, 101.1 us)
Async XLA Ops:
  7.2 17.0 %copy-start = (f32[512,2]{1,0:T(8,128)S(1)}, f32[512,2]{1,0:T(8,128)}, u32[]{:S(2)}) copy-start(f32[512,2]{1,0:T(8,128)} %constant.42.clone.1) | copy-start | bytes 12292
  9.2 30.5 %collective-permute-start.1 = (f32[2,90,1,256]{1,3,2,0:T(8,128)S(1)}, f32[2,90,1,256]{1,3,2,0:T(8,128)S(1)}, u32[]{:S(2)}, u32[]{:S(2)}) collective-permute-start(f32[2,90,1,256]{1,3,2,0:T(8,128)S(1)} %pad_maximum_fusion), channel_id=1, source_target_pairs={{4,0},{8,4},{12,8},{16,12},{20,16},{24,20},{28,24},{32,28},{36,32}... | collective-permute-start | bytes 552968 | tf_op jit(solution)/shard_map/ppermute | solution.py:18
  18.0 21.7 %collective-permute-start = (f32[2,90,1,256]{1,3,2,0:T(8,128)S(1)}, f32[2,90,1,256]{1,3,2,0:T(8,128)S(1)}, u32[]{:S(2)}, u32[]{:S(2)}) collective-permute-start(f32[2,90,1,256]{1,3,2,0:T(8,128)S(1)} %pad_maximum_fusion), channel_id=1, source_target_pairs={{0,4},{4,8},{8,12},{12,16},{16,20},{20,24},{24,28},{28,32},{32,36}... | collective-permute-start | bytes 552968 | tf_op jit(solution)/shard_map/ppermute | solution.py:15
  20.7 19.0 %copy-start.2 = (f32[1,256]{1,0:T(1,128)S(1)}, f32[1,256]{1,0:T(1,128)}, u32[]{:S(2)}) copy-start(f32[1,256]{1,0:T(1,128)} %param.15) | copy-start | bytes 3076
  27.0 25.5 %all-to-all-start.1 = ((f32[128,4,2]{1,2,0:T(2,128)}), f32[128,4,2]{1,2,0:T(2,128)S(1)}, u32[]{:S(2)}, u32[]{:S(2)}) async-start(f32[128,4,2]{1,2,0:T(2,128)} %copy.61), calls=%async_computation.1 | async-start | bytes 262144 | tf_op jit(solution)/shard_map/all_to_all | solution.py:146
  39.9 8.0 %collective-permute-start.3 = (f32[2,90,1,256]{1,3,2,0:T(8,128)S(1)}, f32[2,90,1,256]{1,3,2,0:T(8,128)S(1)}, u32[]{:S(2)}, u32[]{:S(2)}) collective-permute-start(f32[2,90,1,256]{1,3,2,0:T(8,128)S(1)} %fusion.45), channel_id=1, source_target_pairs={{4,0},{8,4},{12,8},{16,12},{20,16},{24,20},{28,24},{32,28},{36,32}... | collective-permute-start | bytes 552968 | tf_op jit(solution)/shard_map/ppermute | solution.py:18
  42.7 6.1 %collective-permute-start.2 = (f32[2,90,1,256]{1,3,2,0:T(8,128)S(1)}, f32[2,90,1,256]{1,3,2,0:T(8,128)S(1)}, u32[]{:S(2)}, u32[]{:S(2)}) collective-permute-start(f32[2,90,1,256]{1,3,2,0:T(8,128)S(1)} %fusion.45), channel_id=1, source_target_pairs={{0,4},{4,8},{8,12},{12,16},{16,20},{20,24},{24,28},{28,32},{32,36}... | collective-permute-start | bytes 552968 | tf_op jit(solution)/shard_map/ppermute | solution.py:15
  45.5 22.7 %copy-start.4 = (f32[56]{0:T(128)S(1)}, f32[56]{0:T(128)}, u32[]{:S(2)}) copy-start(f32[56]{0:T(128)} %param.21) | copy-start | bytes 676
  52.4 15.6 %copy-start.1 = (f32[128,4,2]{1,2,0:T(2,128)}, f32[128,4,2]{1,2,0:T(2,128)S(1)}, u32[]{:S(2)}) copy-start(f32[128,4,2]{1,2,0:T(2,128)S(1)} %all-to-all-done.1) | copy-start | bytes 12292
  52.4 35.8 %all-to-all-start = ((f32[128,4,180]{2,1,0:T(4,128)}), f32[128,4,180]{2,1,0:T(4,128)}, u32[]{:S(2)}, u32[]{:S(2)}) async-start(f32[128,4,180]{2,1,0:T(4,128)} %reshape.191), calls=%async_computation | async-start | bytes 1048576 | tf_op jit(solution)/shard_map/all_to_all | solution.py:145
  68.0 174.1 %all-reduce.2.cloned.1.call-start = ((), (), s32[]{:S(2)}) async-start(), calls=%async_computation.3 | async-start | bytes 524288 | tf_op jit(solution)/shard_map/psum | solution.py:161
  98.4 1.7 copy-start.3
  105.9 1.7 copy-start.3
  113.3 1.7 copy-start.3
  120.7 1.7 copy-start.3
  128.1 1.7 copy-start.3
  135.5 1.7 copy-start.3
  142.9 1.7 copy-start.3
  150.3 1.7 copy-start.3
  157.7 1.7 copy-start.3
  165.1 1.7 copy-start.3
  172.5 1.7 copy-start.3
  179.9 1.7 copy-start.3
  187.3 1.7 copy-start.3
  194.7 1.7 copy-start.3
  242.1 31.7 %all-to-all-start.2 = ((f32[128,4,90]{2,1,0:T(4,128)}), f32[128,4,90]{2,1,0:T(4,128)S(1)}, u32[]{:S(2)}, u32[]{:S(2)}) async-start(f32[128,4,90]{2,1,0:T(4,128)} %all-reduce.2.cloned.1.call-done), calls=%async_computation.2 | async-start | bytes 524288 | tf_op jit(solution)/shard_map/all_to_all | solution.py:162
Sparse Core Ops, SparseCore 0:
  199.4 42.6 all-reduce.1
where the time goes:
time: 286 us; the launch traced here: 283 us
  waiting for transfers between devices  75.5 us (26%)
  starting transfers between devices  61.2 us (21%)
  matrix products  54.1 us (19%)
  local copies, waits for them, and re-layouts  52.1 us (18%)
  other arithmetic  24.2 us (8%)
  between operations  14.3 us (5%)
    psum x1, waiting for transfers between devices, on_device(): summed = lax.psum(partial_value, 'grp')  42.9 us
    dot_general x14, matrix products, layer_pass(): jnp.einsum('lk,gkm->glm', lower_mask, infrared_radiance * growth[:, :stra...  21.2 us
    dot_general x14, matrix products, layer_pass(): jnp.einsum('lk,gkm->glm', upper_mask, infrared_radiance * damped[:, :stra...  19.8 us
    all_to_all x1, starting transfers between devices, on_device(): lax.all_to_all(summed.T.reshape(tile_count, capacity, strata_mesh), 'tile...  16.4 us
    all_to_all x1, starting transfers between devices, on_device(): lax.all_to_all(outgoing, 'tile', split_axis=0, concat_axis=0, tiled=True)  15.6 us
    all_to_all x1, waiting for transfers between devices, on_device(): lax.all_to_all(summed.T.reshape(tile_count, capacity, strata_mesh), 'tile...  14.5 us
    all_to_all x1, waiting for transfers between devices, on_device(): lax.all_to_all(outgoing, 'tile', split_axis=0, concat_axis=0, tiled=True)  14 us
    dot_general x14, matrix products, layer_pass(): jnp.einsum('lk,gkm->glm', lower_mask, thickness, precision=lax.Precision....  13.1 us
  transfers between devices with their start and end apart: 8, of which 6 were waited for; matrix products, arithmetic and copies ran while one was open for 6% of the time, Pallas kernels for 0%

commit v1 on v0

--- a/solution.py
+++ b/solution.py
@@ -158,7 +158,7 @@
         blackbody_share,
         insolation_per_quadrature,
     )
-    summed = lax.psum(partial_value, "grp")
+    summed = jnp.sum(lax.all_gather(partial_value, "grp"), axis=0)
     returning = lax.all_to_all(
         summed.T.reshape(tile_count, capacity, strata_mesh),
         "tile",

time: 286 us -> 234 us (0.82)
  waiting for transfers between devices: 75.5 us -> 32.9 us
  between operations: 14.3 us -> 0.92 us
  blocking collectives: 0 us -> 13.1 us
  starting transfers between devices: 61.2 us -> 51.1 us
    psum x1 -> x0, waiting for transfers between devices: 42.9 us -> none  [on_device(): summed = lax.psum(partial_value, 'grp')]
    all_gather x0 -> x1, blocking collectives: none -> 13.1 us  [on_device(): summed = jnp.sum(lax.all_gather(partial_value, 'grp'), axis=0)]
    all_to_all x1, starting transfers between devices: 16.4 us -> 6.54 us  [on_device(): lax.all_to_all(summed.T.reshape(tile_count, capacity, strata_mesh), 'tile...]
  transfers between devices with their start and end apart: 8 -> 7, of which waited for: 6 -> 5; matrix products, arithmetic and copies ran while one was open for 6% -> 7% of each run, Pallas kernels for 0% -> 0%
where the time goes in v1:
time: 234 us; the launch traced here: 231 us
  matrix products  54.1 us (23%)
  local copies, waits for them, and re-layouts  52.7 us (23%)
  starting transfers between devices  51.1 us (22%)
  waiting for transfers between devices  32.9 us (14%)
  other arithmetic  25 us (11%)
  blocking collectives  13.1 us (6%)
    dot_general x14, matrix products, layer_pass(): jnp.einsum('lk,gkm->glm', lower_mask, infrared_radiance * growth[:, :stra...  21.2 us
    dot_general x14, matrix products, layer_pass(): jnp.einsum('lk,gkm->glm', upper_mask, infrared_radiance * damped[:, :stra...  19.8 us
    all_to_all x1, starting transfers between devices, on_device(): lax.all_to_all(outgoing, 'tile', split_axis=0, concat_axis=0, tiled=True)  15.6 us
    all_to_all x1, waiting for transfers between devices, on_device(): lax.all_to_all(summed.T.reshape(tile_count, capacity, strata_mesh), 'tile...  14.6 us
    all_to_all x1, waiting for transfers between devices, on_device(): lax.all_to_all(outgoing, 'tile', split_axis=0, concat_axis=0, tiled=True)  14.2 us
    dot_general x14, matrix products, layer_pass(): jnp.einsum('lk,gkm->glm', lower_mask, thickness, precision=lax.Precision....  13.1 us
    all_gather x1, blocking collectives, on_device(): summed = jnp.sum(lax.all_gather(partial_value, 'grp'), axis=0)  13.1 us
    all_to_all x1, starting transfers between devices, on_device(): lax.all_to_all(sun_out, 'tile', split_axis=0, concat_axis=0, tiled=True)  12.7 us
  transfers between devices with their start and end apart: 7, of which 5 were waited for; matrix products, arithmetic and copies ran while one was open for 7% of the time, Pallas kernels for 0%

profile of v1, /device:TPU:1, one launch (start us, length us, event | category | flops | bytes accessed | tf_op | source)
XLA Modules:
  0.0 231.3 jit_solution(12192240066263403781)
XLA Ops:
  2.7 8.8 %collective-permute-start.1 = (f32[2,90,1,256]{1,3,2,0:T(8,128)S(1)}, f32[2,90,1,256]{1,3,2,0:T(8,128)S(1)}, u32[]{:S(2)}, u32[]{:S(2)}) collective-permute-start(f32[2,90,1,256]{1,3,2,0:T(8,128)S(1)} %pad_maximum_fusion), channel_id=1, source_target_pairs={{4,0},{8,4},{12,8},{16,12},{20,16},{24,20},{28,24},{32,28},{36,32}... | collective-permute-start | bytes 552968 | tf_op jit(solution)/shard_map/ppermute | solution.py:18
  11.5 1.9 collective-permute-start
  18.9 1.5 copy.74
  20.4 12.7 %all-to-all-start.1 = ((f32[128,4,2]{1,2,0:T(2,128)}), f32[128,4,2]{1,2,0:T(2,128)S(1)}, u32[]{:S(2)}, u32[]{:S(2)}) async-start(f32[128,4,2]{1,2,0:T(2,128)} %copy.74), calls=%async_computation.1 | async-start | bytes 262144 | tf_op jit(solution)/shard_map/all_to_all | solution.py:146
  33.4 2.8 %collective-permute-start.3 = (f32[2,90,1,256]{1,3,2,0:T(8,128)S(1)}, f32[2,90,1,256]{1,3,2,0:T(8,128)S(1)}, u32[]{:S(2)}, u32[]{:S(2)}) collective-permute-start(f32[2,90,1,256]{1,3,2,0:T(8,128)S(1)} %fusion.45), channel_id=1, source_target_pairs={{4,0},{8,4},{12,8},{16,12},{20,16},{24,20},{28,24},{32,28},{36,32}... | collective-permute-start | bytes 552968 | tf_op jit(solution)/shard_map/ppermute | solution.py:18
  36.2 2.8 %collective-permute-start.2 = (f32[2,90,1,256]{1,3,2,0:T(8,128)S(1)}, f32[2,90,1,256]{1,3,2,0:T(8,128)S(1)}, u32[]{:S(2)}, u32[]{:S(2)}) collective-permute-start(f32[2,90,1,256]{1,3,2,0:T(8,128)S(1)} %fusion.45), channel_id=1, source_target_pairs={{0,4},{4,8},{8,12},{12,16},{16,20},{20,24},{24,28},{28,32},{32,36}... | collective-permute-start | bytes 552968 | tf_op jit(solution)/shard_map/ppermute | solution.py:15
  39.0 2.3 %collective-permute-done.3 = f32[2,90,1,256]{1,3,2,0:T(8,128)S(1)} collective-permute-done((f32[2,90,1,256]{1,3,2,0:T(8,128)S(1)}, f32[2,90,1,256]{1,3,2,0:T(8,128)S(1)}, u32[]{:S(2)}, u32[]{:S(2)}) %collective-permute-start.3) | collective-permute-done | bytes 184352 | tf_op jit(solution)/shard_map/ppermute | solution.py:18
  42.4 1.7 scatter_custom_fusion
  46.5 15.6 %all-to-all-start = ((f32[128,4,180]{2,1,0:T(4,128)}), f32[128,4,180]{2,1,0:T(4,128)}, u32[]{:S(2)}, u32[]{:S(2)}) async-start(f32[128,4,180]{2,1,0:T(4,128)} %reshape.191), calls=%async_computation | async-start | bytes 1048576 | tf_op jit(solution)/shard_map/all_to_all | solution.py:145
  64.9 1.6 reshape.189
  68.1 14.2 %all-to-all-done = f32[128,4,180]{2,1,0:T(4,128)} async-done(((f32[128,4,180]{2,1,0:T(4,128)}), f32[128,4,180]{2,1,0:T(4,128)}, u32[]{:S(2)}, u32[]{:S(2)}) %all-to-all-start) | async-done | bytes 368672 | tf_op jit(solution)/shard_map/all_to_all | solution.py:145
  82.3 2.0 reshape.192
  84.3 2.0 slice_bitcast_fusion
  88.5 103.7 %while.12 = (s32[]{:T(128)}, f32[14,90,512]{2,1,0:T(8,128)S(1)}, f32[14,4,90]{2,1,0:T(4,128)}, f32[14,4]{1,0:T(8,128)S(1)}, f32[14,4,512]{2,1,0:T(4,128)}, /*ind...) while((s32[]{:T(128)}, f32[14,90,512]{2,1,0:T(8,128)S(1)}, ...), condition=%wide.region_7.8_spmd.clone.clone, body=%wide.region_5.7_spmd.clone.clone.sunk | while | flops 608476160 | bytes 12221821 | solution.py:78
  94.3 1.5 fusion.81
  101.7 1.5 fusion.81
  107.6 1.4 fusion.79
  109.1 1.5 fusion.81
  116.5 1.5 fusion.81
  123.9 1.5 fusion.81
  131.3 1.5 fusion.81
  138.7 1.5 fusion.81
  146.1 1.5 fusion.81
  153.5 1.5 fusion.81
  160.9 1.5 fusion.81
  168.3 1.5 fusion.81
  175.7 1.5 fusion.81
  183.1 1.5 fusion.81
  190.5 1.5 fusion.81
  193.1 13.1 %all-gather.1 = f32[4,90,512]{2,1,0:T(8,128)S(1)} all-gather(f32[1,90,512]{2,1,0:T(8,128)} %bitcast.145), channel_id=2, replica_groups=mesh['tile'=128,'grp'=4] {'grp'}, dimensions={0}, use_global_device_ids=true | all-gather | bytes 921600 | tf_op jit(solution)/shard_map/all_gather | solution.py:161
  207.1 6.5 %all-to-all-start.2 = ((f32[128,4,90]{2,1,0:T(4,128)}), f32[128,4,90]{2,1,0:T(4,128)S(1)}, u32[]{:S(2)}, u32[]{:S(2)}) async-start(f32[128,4,90]{2,1,0:T(4,128)} %bitcast.22), calls=%async_computation.2 | async-start | bytes 524288 | tf_op jit(solution)/shard_map/all_to_all | solution.py:162
  214.4 14.6 %all-to-all-done.2 = f32[128,4,90]{2,1,0:T(4,128)S(1)} async-done(((f32[128,4,90]{2,1,0:T(4,128)}), f32[128,4,90]{2,1,0:T(4,128)S(1)}, u32[]{:S(2)}, u32[]{:S(2)}) %all-to-all-start.2) | async-done | bytes 184352 | tf_op jit(solution)/shard_map/all_to_all | solution.py:162
  (264 shorter events, 102.2 us)
Async XLA Ops:
  0.6 17.0 %copy-start = (f32[512,2]{1,0:T(8,128)S(1)}, f32[512,2]{1,0:T(8,128)}, u32[]{:S(2)}) copy-start(f32[512,2]{1,0:T(8,128)} %constant.42.clone.1) | copy-start | bytes 12292
  2.7 30.5 %collective-permute-start.1 = (f32[2,90,1,256]{1,3,2,0:T(8,128)S(1)}, f32[2,90,1,256]{1,3,2,0:T(8,128)S(1)}, u32[]{:S(2)}, u32[]{:S(2)}) collective-permute-start(f32[2,90,1,256]{1,3,2,0:T(8,128)S(1)} %pad_maximum_fusion), channel_id=1, source_target_pairs={{4,0},{8,4},{12,8},{16,12},{20,16},{24,20},{28,24},{32,28},{36,32}... | collective-permute-start | bytes 552968 | tf_op jit(solution)/shard_map/ppermute | solution.py:18
  11.5 21.7 %collective-permute-start = (f32[2,90,1,256]{1,3,2,0:T(8,128)S(1)}, f32[2,90,1,256]{1,3,2,0:T(8,128)S(1)}, u32[]{:S(2)}, u32[]{:S(2)}) collective-permute-start(f32[2,90,1,256]{1,3,2,0:T(8,128)S(1)} %pad_maximum_fusion), channel_id=1, source_target_pairs={{0,4},{4,8},{8,12},{12,16},{16,20},{20,24},{24,28},{28,32},{32,36}... | collective-permute-start | bytes 552968 | tf_op jit(solution)/shard_map/ppermute | solution.py:15
  14.2 19.0 %copy-start.2 = (f32[1,256]{1,0:T(1,128)S(1)}, f32[1,256]{1,0:T(1,128)}, u32[]{:S(2)}) copy-start(f32[1,256]{1,0:T(1,128)} %param.15) | copy-start | bytes 3076
  20.4 25.5 %all-to-all-start.1 = ((f32[128,4,2]{1,2,0:T(2,128)}), f32[128,4,2]{1,2,0:T(2,128)S(1)}, u32[]{:S(2)}, u32[]{:S(2)}) async-start(f32[128,4,2]{1,2,0:T(2,128)} %copy.74), calls=%async_computation.1 | async-start | bytes 262144 | tf_op jit(solution)/shard_map/all_to_all | solution.py:146
  33.4 8.0 %collective-permute-start.3 = (f32[2,90,1,256]{1,3,2,0:T(8,128)S(1)}, f32[2,90,1,256]{1,3,2,0:T(8,128)S(1)}, u32[]{:S(2)}, u32[]{:S(2)}) collective-permute-start(f32[2,90,1,256]{1,3,2,0:T(8,128)S(1)} %fusion.45), channel_id=1, source_target_pairs={{4,0},{8,4},{12,8},{16,12},{20,16},{24,20},{28,24},{32,28},{36,32}... | collective-permute-start | bytes 552968 | tf_op jit(solution)/shard_map/ppermute | solution.py:18
  36.2 6.1 %collective-permute-start.2 = (f32[2,90,1,256]{1,3,2,0:T(8,128)S(1)}, f32[2,90,1,256]{1,3,2,0:T(8,128)S(1)}, u32[]{:S(2)}, u32[]{:S(2)}) collective-permute-start(f32[2,90,1,256]{1,3,2,0:T(8,128)S(1)} %fusion.45), channel_id=1, source_target_pairs={{0,4},{4,8},{8,12},{12,16},{16,20},{20,24},{24,28},{28,32},{32,36}... | collective-permute-start | bytes 552968 | tf_op jit(solution)/shard_map/ppermute | solution.py:15
  39.0 23.2 %copy-start.4 = (f32[56]{0:T(128)S(1)}, f32[56]{0:T(128)}, u32[]{:S(2)}) copy-start(f32[56]{0:T(128)} %param.21) | copy-start | bytes 676
  45.9 0.6 copy-start.1
  46.5 35.8 %all-to-all-start = ((f32[128,4,180]{2,1,0:T(4,128)}), f32[128,4,180]{2,1,0:T(4,128)}, u32[]{:S(2)}, u32[]{:S(2)}) async-start(f32[128,4,180]{2,1,0:T(4,128)} %reshape.191), calls=%async_computation | async-start | bytes 1048576 | tf_op jit(solution)/shard_map/all_to_all | solution.py:145
  92.5 1.7 copy-start.3
  99.9 1.7 copy-start.3
  107.3 1.7 copy-start.3
  114.8 1.7 copy-start.3
  122.2 1.7 copy-start.3
  129.6 1.7 copy-start.3
  137.0 1.7 copy-start.3
  144.4 1.7 copy-start.3
  151.8 1.7 copy-start.3
  159.2 1.7 copy-start.3
  166.6 1.7 copy-start.3
  174.0 1.7 copy-start.3
  181.4 1.7 copy-start.3
  188.8 1.7 copy-start.3
  207.1 21.9 %all-to-all-start.2 = ((f32[128,4,90]{2,1,0:T(4,128)}), f32[128,4,90]{2,1,0:T(4,128)S(1)}, u32[]{:S(2)}, u32[]{:S(2)}) async-start(f32[128,4,90]{2,1,0:T(4,128)} %bitcast.22), calls=%async_computation.2 | async-start | bytes 524288 | tf_op jit(solution)/shard_map/all_to_all | solution.py:162
